TPU v7x, 768 devices: a whole 4x8x12 slice. The times are simulated.
768 devices in a mesh: rep: 48 (over x, z), shard: 16 (over y, core).
Axes of the slice: x: 4, y: 8, z: 12, core: 2. Of those that a mesh axis runs over, the one named last changes fastest.
Arguments:
- cotangent: bfloat16 [98304, 1024], P(('rep', 'shard')), may hold values from -0.3984375 to 0.3984375
- pooled: bfloat16 [98304, 8, 128], P(('rep', 'shard')), may hold values from -6 to 6
- fm_weight: bfloat16 [64, 1024], replicated, may hold values from -0.1875 to 0.1875
- row_ids: int32 [768, 8, 192], P(('rep', 'shard')), may hold values from 0 to 9215, as said below
- bag_offsets: int32 [768, 8, 128], P(('rep', 'shard')), may hold values from 0 to 191, as said below
- table: float32 [8, 9216, 128], P(None, 'shard'), may hold values from -3 to 3
- accum: float32 [8, 9216], P(None, 'shard'), may hold values from 0.2 to 4
Outputs:
- new_table: float32 [8, 9216, 128], P(None, 'shard')
- new_accum: float32 [8, 9216], P(None, 'shard')
Inputs may be any that keep to these rules, and one draw needn't show every extreme that they name: `row_ids`: for each device and table, at most 24 ids have the same value of id // 576, and exactly 24 for one such value. `bag_offsets`: each row starts at 0 and rises by 1 or 2 from one sample to the next; the last bag ends at 192.
All inputs are finite; a program needn't handle non-finite values.
Results may differ from a plain program's by a relative error of at most 0.006.
Values may be sent and summed in bfloat16 or wider, within the bound.
A program may use at most 32 MiB of HBM per device.

v0:
```python
import jax
import jax.numpy as jnp
from jax import lax
from jax.sharding import PartitionSpec as P

LEARN = 0.5


def fm_backward(cotangent, pooled, fm_weight):
    batch = pooled.shape[0]
    tables = pooled.shape[1]
    width = pooled.shape[2]
    dz = lax.dot_general(
        cotangent, fm_weight, (((1,), (1,)), ((), ())), preferred_element_type=jnp.float32
    )
    dz = dz.reshape(batch, tables, tables)
    symmetric = dz + jnp.swapaxes(dz, 1, 2)
    grad = cotangent.astype(jnp.float32).reshape(batch, tables, width)
    grad = grad + jnp.einsum("bij,bje->bie", symmetric, pooled.astype(jnp.float32))
    return grad.astype(jnp.bfloat16)


def bucket_rows(pooled_grad, ids, offsets, rows_dev, groups, capacity):
    tables = ids.shape[0]
    look = ids.shape[1]
    width = pooled_grad.shape[2]
    position = lax.iota(jnp.int32, look)
    inside = (offsets[:, None, :] <= position[None, :, None]).astype(jnp.int32)
    sample = jnp.sum(inside, axis=2) - 1
    owner = ids // rows_dev
    local = ids - owner * rows_dev
    member = (owner[:, :, None] == lax.iota(jnp.int32, groups)[None, None, :]).astype(jnp.int32)
    before = jnp.cumsum(member, axis=1) - member
    slot = owner * capacity + jnp.sum(before * member, axis=2)
    table_index = lax.iota(jnp.int32, tables)[:, None]
    values = pooled_grad[sample, table_index]
    payload = (
        jnp.zeros((tables, groups * capacity, width), jnp.bfloat16)
        .at[table_index, slot]
        .set(values)
    )
    targets = jnp.full((tables, groups * capacity), -1, jnp.int32).at[table_index, slot].set(local)
    return (payload, targets)


def scatter_rows(payload, targets, rows_dev):
    row_index = lax.iota(jnp.int32, rows_dev)
    onehot = (targets[:, None, :] == row_index[None, :, None]).astype(jnp.bfloat16)
    return jnp.einsum("trs,tse->tre", onehot, payload, preferred_element_type=jnp.float32)


def adagrad(table, accum, grad):
    accum_new = accum + jnp.mean(grad * grad, axis=2)
    return (table - LEARN * grad / jnp.sqrt(accum_new)[..., None], accum_new)


def on_device(cotangent, pooled, fm_weight, row_ids, bag_offsets, table, accum):
    groups = lax.axis_size("shard")
    rows_dev = table.shape[1]
    look = row_ids.shape[2]
    capacity = 2 * look // groups
    pooled_grad = fm_backward(cotangent, pooled, fm_weight)
    payload, targets = bucket_rows(
        pooled_grad, row_ids[0], bag_offsets[0], rows_dev, groups, capacity
    )
    arrived, arrived_rows = (
        lax.all_to_all(payload, "shard", split_axis=1, concat_axis=1, tiled=True),
        lax.all_to_all(targets, "shard", split_axis=1, concat_axis=1, tiled=True),
    )
    grad = scatter_rows(arrived, arrived_rows, rows_dev)
    total = lax.psum(grad, "rep")
    return adagrad(table, accum, total)


def solution(mesh):
    return jax.shard_map(
        on_device,
        mesh=mesh,
        in_specs=(
            P(("rep", "shard"), None),
            P(("rep", "shard"), None, None),
            P(),
            P(("rep", "shard"), None, None),
            P(("rep", "shard"), None, None),
            P(None, "shard", None),
            P(None, "shard"),
        ),
        out_specs=(P(None, "shard", None), P(None, "shard")),
        check_vma=False,
    )
```

profile of v0, /device:TPU:8, one launch (start us, length us, event | category | flops | bytes accessed | tf_op | source)
XLA Modules:
  0.0 324.7 jit_solution(1478310385345238271)
XLA Ops:
  7.2 0.8 bitcast_subtract_fusion
  8.1 4.6 %reduce-window.6 = s32[8,16,2,128]{3,1,2,0:T(8,128)S(1)} reduce-window(s32[8,16,2,128]{3,1,2,0:T(8,128)S(1)} %copy_bitcast_fusion, s32[]{:T(128)} %constant.15.clone.1), window={size=1x1x1x128 pad=0_0x0_0x0_0x127_0}, to_apply=%region_0.0 | reduce-window | flops 4161536 | bytes 262148 | tf_op jit(solution)/shard_map/reduce-window
  12.6 0.1 slice.14
  12.7 0.2 copy.35
  13.0 0.1 bitcast_bitcast_fusion
  13.2 0.7 compare_select_fusion.1
  13.9 0.7 and_reduce_fusion
  14.6 0.7 multiply_reduce_fusion.1
  15.4 0.1 reshape.154
  15.4 6.2 %scatter_custom_fusion = s32[3072]{0:T(1024)S(1)} fusion(s32[1536]{0:T(1024)S(1)} %reshape.154, s32[1536]{0:T(1024)S(1)} %reshape.156, s32[]{:T(128)} %constant.12.clone.1), kind=kCustom, calls=%fused_computation.54 | custom fusion | bytes 12292
  21.6 0.1 all_to_all.9
  21.7 0.7 reshape.176
  22.5 12.8 %all-to-all-start = ((s32[16,1,192]{2,1,0:T(1,128)}), s32[16,1,192]{2,1,0:T(1,128)S(1)}, u32[]{:S(2)}, u32[]{:S(2)}) async-start(s32[16,1,192]{2,1,0:T(1,128)} %reshape.176), calls=%async_computation | async-start | bytes 32768 | tf_op jit(solution)/shard_map/all_to_all | solution.py:68
  35.2 1.2 convolution_bitcast_fusion
  36.4 0.2 copy.41
  36.6 0.2 copy.40
  37.0 0.4 convert_reduce_fusion
  37.3 0.1 copy.46
  37.4 0.3 fusion.2
  37.8 11.7 %scatter_custom_fusion.1 = bf16[3072,128]{1,0:T(8,128)(2,1)S(1)} fusion(s32[1536]{0:T(1024)S(1)} %reshape.154, bf16[128,8,128]{2,1,0:T(8,128)(2,1)S(1)} %fusion.2, s32[1536]{0:T(1024)S(1)} %reshape.148, bf16[]{:T(256)} %constant.37.clone.1), kind=kCustom, calls=%fused_computation.16 | custom fusion | bytes 786434
  49.6 1.4 copy.42
  51.0 7.3 %all-to-all-start.1 = ((bf16[8,384,128]{2,0,1:T(8,128)(2,1)}), bf16[8,384,128]{2,0,1:T(8,128)(2,1)S(1)}, u32[]{:S(2)}, u32[]{:S(2)}) async-start(bf16[8,384,128]{2,0,1:T(8,128)(2,1)} %copy.42), calls=%async_computation.1 | async-start | bytes 1572864 | tf_op jit(solution)/shard_map/all_to_all | solution.py:67
  58.3 0.5 broadcast.192
  58.8 0.7 reduce.6
  59.5 0.1 reshape.177
  59.6 0.1 eq.41
  59.7 17.6 %all-to-all-done.1 = bf16[8,384,128]{2,0,1:T(8,128)(2,1)S(1)} async-done(((bf16[8,384,128]{2,0,1:T(8,128)(2,1)}), bf16[8,384,128]{2,0,1:T(8,128)(2,1)S(1)}, u32[]{:S(2)}, u32[]{:S(2)}) %all-to-all-start.1) | async-done | bytes 786464 | tf_op jit(solution)/shard_map/all_to_all | solution.py:67
  77.3 2.8 fusion
  80.1 232.6 %all-reduce.3.cloned.1.call-done = f32[8,576,128]{2,1,0:T(8,128)} async-done(((f32[8,576,128]{2,1,0:T(8,128)}), f32[8,576,128]{2,1,0:T(8,128)}) %all-reduce.3.cloned.1.call-update) | async-done | bytes 2359312 | tf_op jit(solution)/shard_map/psum | solution.py:71
  312.7 2.6 multiply_reduce_fusion
  315.3 0.6 fusion.23
  315.9 1.9 divide_subtract_fusion
  (29 shorter events, 0.5 us)
Async XLA Ops:
  7.2 30.3 %copy-start = (bf16[128,8,128]{2,1,0:T(8,128)(2,1)S(1)}, bf16[128,8,128]{2,1,0:T(8,128)(2,1)}, u32[]{:S(2)}) copy-start(bf16[128,8,128]{2,1,0:T(8,128)(2,1)} %param.8) | copy-start | bytes 786436
  7.2 29.7 %copy-start.3 = (bf16[128,1024]{1,0:T(8,128)(2,1)S(1)}, bf16[128,1024]{1,0:T(8,128)(2,1)}, u32[]{:S(2)}) copy-start(bf16[128,1024]{1,0:T(8,128)(2,1)} %param.7) | copy-start | bytes 786436
  7.2 29.8 %copy-start.5 = (s32[1,8,128]{2,1,0:T(8,128)S(1)}, s32[1,8,128]{2,1,0:T(8,128)}, u32[]{:S(2)}) copy-start(s32[1,8,128]{2,1,0:T(8,128)} %param.11) | copy-start | bytes 12292
  22.5 28.5 %all-to-all-start = ((s32[16,1,192]{2,1,0:T(1,128)}), s32[16,1,192]{2,1,0:T(1,128)S(1)}, u32[]{:S(2)}, u32[]{:S(2)}) async-start(s32[16,1,192]{2,1,0:T(1,128)} %reshape.176), calls=%async_computation | async-start | bytes 32768 | tf_op jit(solution)/shard_map/all_to_all | solution.py:68
  51.0 26.3 %all-to-all-start.1 = ((bf16[8,384,128]{2,0,1:T(8,128)(2,1)}), bf16[8,384,128]{2,0,1:T(8,128)(2,1)S(1)}, u32[]{:S(2)}, u32[]{:S(2)}) async-start(bf16[8,384,128]{2,0,1:T(8,128)(2,1)} %copy.42), calls=%async_computation.1 | async-start | bytes 1572864 | tf_op jit(solution)/shard_map/all_to_all | solution.py:67
  58.2 254.5 %all-reduce.3.cloned.1.call-start = ((), (), s32[]{:S(2)}) async-start(), calls=%async_computation.2 | async-start | bytes 4718592 | tf_op jit(solution)/shard_map/psum | solution.py:71
  80.1 235.2 %copy-start.4 = (f32[8,576]{1,0:T(8,128)S(1)}, f32[8,576]{1,0:T(8,128)}, u32[]{:S(2)}) copy-start(f32[8,576]{1,0:T(8,128)} %param.13) | copy-start | bytes 55300
  80.1 235.8 %copy-start.2 = (f32[8,576,128]{2,1,0:T(8,128)S(1)}, f32[8,576,128]{2,1,0:T(8,128)}, u32[]{:S(2)}) copy-start(f32[8,576,128]{2,1,0:T(8,128)} %param.12) | copy-start | bytes 7077892
  312.7 3.2 copy-start.1
Sparse Core Ops, SparseCore 0:
  80.3 232.3 all-reduce.2
where the time goes:
time: 325 us
  waiting for transfers between devices  250 us (77%)
  local copies, waits for them, and re-layouts  21.9 us (7%)
  starting transfers between devices  20 us (6%)
  between operations  14.3 us (4%)
  other arithmetic  13.9 us (4%)
  matrix products  4.26 us (1%)
    psum x1, waiting for transfers between devices, on_device(): total = lax.psum(grad, 'rep')  233 us
    unnamed x18, local copies, waits for them, and re-layouts  18.9 us
    all_to_all x1, waiting for transfers between devices, on_device(): lax.all_to_all(payload, 'shard', split_axis=1, concat_axis=1, tiled=True)  17.6 us
    all_to_all x1, starting transfers between devices, on_device(): lax.all_to_all(targets, 'shard', split_axis=1, concat_axis=1, tiled=True)  12.8 us
    all_to_all x1, starting transfers between devices, on_device(): lax.all_to_all(payload, 'shard', split_axis=1, concat_axis=1, tiled=True)  7.26 us
  transfers between devices with their start and end apart: 3, of which 2 were waited for; matrix products, arithmetic and copies ran while one was open for 5% of the time, Pallas kernels for 0%

commit v1 on v0

v1 whole, which is shorter than its diff:
```python
import functools

import jax
import jax.numpy as jnp
from jax import lax
from jax.experimental import pallas as pl
from jax.experimental.pallas import tpu as pltpu
from jax.sharding import PartitionSpec as P

LEARN = 0.5
NX, NZ, NY = 4, 12, 8
GROUPS = 2 * NY
TBL, E, B_DEV, LOOK, CAP, ROWS_DEV = 8, 128, 128, 192, 24, 576
SLOTS = GROUPS * CAP
HEAD = 16
PAIRS = TBL // 2
PAIR_ROWS = 2 * CAP
MSG = HEAD + PAIRS * PAIR_ROWS
HALVES = TBL // NX
CUT = ROWS_DEV // 2
PIECE = ROWS_DEV // NZ
BF, F32, I32 = jnp.bfloat16, jnp.float32, jnp.int32


def iota(shape, dim):
    return lax.broadcasted_iota(I32, shape, dim)


def dot(a, b, dims=((1,), (0,))):
    return lax.dot_general(a, b, (dims, ((), ())), preferred_element_type=F32)


def shard_offsets():
    order = []
    for dy in (4, 3, 5, 2, 6, 1, 7, 0):
        for dc in (0, 1):
            if (dy, dc) != (0, 0):
                order.append((dy, dc))
    return order


def exchange_kernel(
    cot_ref, x_ref, w_ref, ids_ref, off_ref, out_ref,
    send, recv, pg, tgt, dense, relay, relay_out, xin, xsum, zin,
    a2a_s, a2a_r, x1_s, x1_r, x2_s, x2_r, z_s, z_r, zg_s, zg_r, xg_s, xg_r, xf_s, xf_r,
):
    rep = lax.axis_index("rep")
    sh = lax.axis_index("shard")
    mx, mz = rep // NZ, rep % NZ
    my, mc = sh // 2, sh % 2

    def shard_peer(dy, dc):
        return {"rep": rep, "shard": lax.rem(my + dy, NY) * 2 + lax.rem(mc + dc, 2)}

    def x_peer(d):
        return {"rep": lax.rem(mx + d, NX) * NZ + mz, "shard": sh}

    def z_peer(d):
        return {"rep": mx * NZ + lax.rem(mz + d, NZ), "shard": sh}

    barrier = pltpu.get_barrier_semaphore()
    partners = [shard_peer(dy, dc) for dy, dc in shard_offsets()]
    partners += [x_peer(1), x_peer(NX - 1)] + [z_peer(d) for d in range(1, NZ)]
    for peer in partners:
        pl.semaphore_signal(barrier, inc=1, device_id=peer, device_id_type=pl.DeviceIdType.MESH)

    swap = (iota((64, 64), 1) == (iota((64, 64), 0) % 8) * 8 + iota((64, 64), 0) // 8).astype(BF)
    w = w_ref[...]
    w_t = dot(swap, w).astype(BF)
    cot = cot_ref[...]
    sym = dot(cot, w, ((1,), (1,))) + dot(cot, w_t, ((1,), (1,)))
    for i in range(TBL):
        acc = cot_ref[:, i * E:(i + 1) * E].astype(F32)
        for j in range(TBL):
            acc = acc + sym[:, i * TBL + j:i * TBL + j + 1] * x_ref[:, j * E:(j + 1) * E].astype(F32)
        pg[i] = acc.astype(BF)

    ids = ids_ref[...]
    owner = lax.shift_right_logical(ids * 7282, 22)
    local = ids - owner * ROWS_DEV + 1
    rel = ((lax.shift_right_logical(owner, 1) - my) & (NY - 1)) * 2 + ((owner & 1) ^ mc)
    member = jnp.concatenate(
        [(rel[t:t + 1, :] == iota((GROUPS, LOOK), 0)).astype(F32) for t in range(TBL)], axis=0
    )
    earlier = (iota((LOOK, LOOK), 0) < iota((LOOK, LOOK), 1)).astype(BF)
    before = dot(member.astype(BF), earlier)
    rank = jnp.sum((member * before).reshape(TBL, GROUPS, LOOK), axis=1).astype(I32)
    slot = rel * CAP + rank
    high = lax.shift_right_logical(local, 5).astype(F32)
    low = (local & 31).astype(F32)
    after = pltpu.roll(off_ref[...], B_DEV - 1, 1)
    after = jnp.where(iota((TBL, B_DEV), 1) == B_DEV - 1, LOOK, after)

    def spread(t):
        return (iota((SLOTS, LOOK), 0) == slot[t:t + 1, :]).astype(BF)

    rows_h, rows_l = [], []
    for t in range(TBL):
        hl = jnp.where(iota((8, LOOK), 0) == 0, high[t:t + 1, :], low[t:t + 1, :]).astype(BF)
        placed = dot(hl, spread(t), ((1,), (1,)))
        rows_h.append(placed[0:1, :])
        rows_l.append(placed[1:2, :])
    targets = jnp.concatenate(rows_h + rows_l, axis=0)
    mine = (iota((GROUPS, 1, SLOTS), 2) // CAP == iota((GROUPS, 1, SLOTS), 0)).astype(F32)
    fold = (iota((E, SLOTS), 1) % CAP == iota((E, SLOTS), 0)).astype(BF)
    apart = (targets[None] * mine).astype(BF).reshape(GROUPS * HEAD, SLOTS)
    send[:, 0:HEAD, :] = dot(apart, fold, ((1,), (1,))).astype(BF).reshape(GROUPS, HEAD, E)
    recv[0, 0:HEAD, :] = send[0, 0:HEAD, :]

    def a2a(p, dy, dc):
        o = dy * 2 + dc
        first = 0 if p == 0 else HEAD + PAIR_ROWS * p
        rows = pl.ds(first, HEAD + PAIR_ROWS * (p + 1) - first)
        return pltpu.make_async_remote_copy(
            send.at[o, rows], recv.at[o, rows], a2a_s.at[p, o], a2a_r.at[p, o],
            device_id=shard_peer(dy, dc), device_id_type=pl.DeviceIdType.MESH,
        )

    kpos = iota((LOOK, B_DEV), 0)
    sends = []
    for p in range(PAIRS):
        parts = []
        for t in (2 * p, 2 * p + 1):
            bags = ((kpos >= off_ref[t:t + 1, :]) & (kpos < after[t:t + 1, :])).astype(BF)
            values = dot(bags, pg[t]).astype(BF)
            parts.append(dot(spread(t), values).reshape(GROUPS, CAP, E))
        both = jnp.concatenate(parts, axis=1).astype(BF)
        rows = slice(HEAD + PAIR_ROWS * p, HEAD + PAIR_ROWS * (p + 1))
        send[:, rows, :] = both
        recv[0, rows, :] = both[0]
        if p == 0:
            pl.semaphore_wait(barrier, len(partners))
        for dy, dc in shard_offsets():
            copy = a2a(p, dy, dc)
            copy.start()
            sends.append(copy)

    def scatter(p):
        for dy, dc in shard_offsets():
            a2a(p, dy, dc).wait_recv()
        if p == 0:
            heads = dot(recv[:, 0:HEAD, :].reshape(GROUPS * HEAD, E), fold).reshape(GROUPS, HEAD, SLOTS)
            got = jnp.sum(heads * mine, axis=0)
            tgt[...] = (got[0:TBL] * 32.0 + got[TBL:2 * TBL]).astype(I32) - 1
        rows = slice(HEAD + PAIR_ROWS * p, HEAD + PAIR_ROWS * (p + 1))
        both = recv[:, rows, :].astype(F32)
        for a in range(2):
            t = 2 * p + a
            values = both[:, a * CAP:(a + 1) * CAP, :].reshape(SLOTS, E).astype(BF)
            onehot = (iota((ROWS_DEV, SLOTS), 0) == tgt[t:t + 1, :]).astype(BF)
            dense[t] = dot(onehot, values).astype(BF)

    upper, lower = pl.ds(0, CUT), pl.ds(CUT, CUT)

    def table(h, d):
        return h * NX + lax.rem(mx + d, NX)

    def remote(src, dst, s, r, peer):
        return pltpu.make_async_remote_copy(
            src, dst, s, r, device_id=peer, device_id_type=pl.DeviceIdType.MESH
        )

    right, left = x_peer(1), x_peer(NX - 1)

    def x_first(h):
        t2, t1, t3 = table(h, 2), table(h, 1), table(h, 3)
        return [
            remote(dense.at[t2, upper], relay.at[h, 0], x1_s.at[h, 0], x1_r.at[h, 0], right),
            remote(dense.at[t2, lower], relay.at[h, 1], x1_s.at[h, 1], x1_r.at[h, 1], left),
            remote(dense.at[t1, lower], xin.at[h, 0, lower], x1_s.at[h, 2], x1_r.at[h, 2], right),
            remote(dense.at[t3, upper], xin.at[h, 1, upper], x1_s.at[h, 3], x1_r.at[h, 3], left),
        ]

    def x_second(h):
        return [
            remote(relay_out.at[h, 0], xin.at[h, 0, upper], x2_s.at[h, 0], x2_r.at[h, 0], right),
            remote(relay_out.at[h, 1], xin.at[h, 1, lower], x2_s.at[h, 1], x2_r.at[h, 1], left),
        ]

    def z_reduce(h):
        copies = []
        for d in range(1, NZ):
            w_at = lax.rem(mz + d, NZ)
            rows = pl.ds(pl.multiple_of(w_at * PIECE, PIECE), PIECE)
            copies.append(remote(xsum.at[h, rows], zin.at[h, d], z_s.at[h, d], z_r.at[h, d], z_peer(d)))
        return copies

    own_rows = pl.ds(pl.multiple_of(mz * PIECE, PIECE), PIECE)

    def z_gather(h):
        t0 = table(h, 0)
        return [
            remote(out_ref.at[t0, own_rows], out_ref.at[t0, own_rows], zg_s.at[h, d], zg_r.at[h, d], z_peer(d))
            for d in range(1, NZ)
        ]

    def z_gather_wait(h):
        t0 = table(h, 0)
        for d in range(1, NZ):
            at = pl.ds(pl.multiple_of(lax.rem(mz + NZ - d, NZ) * PIECE, PIECE), PIECE)
            remote(out_ref.at[t0, at], out_ref.at[t0, at], zg_s.at[h, d], zg_r.at[h, d], z_peer(d)).wait_recv()

    def x_gather(h, d):
        t0 = table(h, d)
        return [
            remote(out_ref.at[t0, upper], out_ref.at[t0, upper], xg_s.at[h, 0], xg_r.at[h, 0], right),
            remote(out_ref.at[t0, lower], out_ref.at[t0, lower], xg_s.at[h, 1], xg_r.at[h, 1], left),
            remote(out_ref.at[t0, lower], out_ref.at[t0, lower], xg_s.at[h, 2], xg_r.at[h, 2], right),
            remote(out_ref.at[t0, upper], out_ref.at[t0, upper], xg_s.at[h, 3], xg_r.at[h, 3], left),
        ]

    def x_forward(h, d0, d1):
        ta, tb = table(h, d0), table(h, d1)
        return [
            remote(out_ref.at[ta, upper], out_ref.at[ta, upper], xf_s.at[h, 0], xf_r.at[h, 0], right),
            remote(out_ref.at[tb, lower], out_ref.at[tb, lower], xf_s.at[h, 1], xf_r.at[h, 1], left),
        ]

    def start(copies):
        for copy in copies:
            copy.start()
        sends.extend(copies)

    def do_scatter(h):
        for p in range(h * NX // 2, (h + 1) * NX // 2):
            scatter(p)
        start(x_first(h))

    def do_relay(h):
        first, second = x_first(h), x_second(h)
        first[0].wait_recv()
        relay_out[h, 0] = (relay[h, 0].astype(F32) + dense[table(h, 1), upper].astype(F32)).astype(BF)
        start(second[0:1])
        first[1].wait_recv()
        relay_out[h, 1] = (relay[h, 1].astype(F32) + dense[table(h, 3), lower].astype(F32)).astype(BF)
        start(second[1:2])

    def do_x_sum(h):
        first, second = x_first(h), x_second(h)
        for copy in (first[2], first[3], second[0], second[1]):
            copy.wait_recv()
        total = dense[table(h, 0)].astype(F32) + xin[h, 0].astype(F32) + xin[h, 1].astype(F32)
        xsum[h] = total.astype(BF)
        start(z_reduce(h))

    def do_z_sum(h):
        total = xsum[h, own_rows].astype(F32)
        for d, copy in enumerate(z_reduce(h), start=1):
            copy.wait_recv()
            total = total + zin[h, d].astype(F32)
        out_ref[table(h, 0), own_rows] = total.astype(BF)
        start(z_gather(h))

    def do_x_gather(h):
        z_gather_wait(h)
        start(x_gather(h, 0))

    def do_forward(h):
        from_left, from_right = x_gather(h, 3), x_gather(h, 1)
        forward = x_forward(h, 3, 1)
        from_left[0].wait_recv()
        start(forward[0:1])
        from_right[1].wait_recv()
        start(forward[1:2])

    def do_end(h):
        x_gather(h, 3)[2].wait_recv()
        x_gather(h, 1)[3].wait_recv()
        for copy in x_forward(h, 2, 2):
            copy.wait_recv()

    do_scatter(0)
    do_relay(0)
    do_x_sum(0)
    do_scatter(1)
    do_z_sum(0)
    do_relay(1)
    do_x_gather(0)
    do_x_sum(1)
    do_forward(0)
    do_z_sum(1)
    do_end(0)
    do_x_gather(1)
    do_forward(1)
    do_end(1)
    for copy in sends:
        copy.wait_send()


def exchange(cot, pooled, w, ids, offsets):
    vmem = pl.BlockSpec(memory_space=pltpu.VMEM)
    dma = pltpu.SemaphoreType.DMA
    return pl.pallas_call(
        exchange_kernel,
        out_shape=jax.ShapeDtypeStruct((TBL, ROWS_DEV, E), BF),
        in_specs=[vmem] * 5,
        out_specs=vmem,
        scratch_shapes=[
            pltpu.VMEM((GROUPS, MSG, E), BF),
            pltpu.VMEM((GROUPS, MSG, E), BF),
            pltpu.VMEM((TBL, B_DEV, E), BF),
            pltpu.VMEM((TBL, SLOTS), I32),
            pltpu.VMEM((TBL, ROWS_DEV, E), BF),
            pltpu.VMEM((HALVES, 2, CUT, E), BF),
            pltpu.VMEM((HALVES, 2, CUT, E), BF),
            pltpu.VMEM((HALVES, 2, ROWS_DEV, E), BF),
            pltpu.VMEM((HALVES, ROWS_DEV, E), BF),
            pltpu.VMEM((HALVES, NZ, PIECE, E), BF),
            dma((PAIRS, GROUPS)), dma((PAIRS, GROUPS)),
            dma((HALVES, 4)), dma((HALVES, 4)),
            dma((HALVES, 2)), dma((HALVES, 2)),
            dma((HALVES, NZ)), dma((HALVES, NZ)),
            dma((HALVES, NZ)), dma((HALVES, NZ)),
            dma((HALVES, 4)), dma((HALVES, 4)),
            dma((HALVES, 2)), dma((HALVES, 2)),
        ],
        compiler_params=pltpu.CompilerParams(
            collective_id=0, has_side_effects=True, vmem_limit_bytes=40 * 1024 * 1024
        ),
    )(cot, pooled, w, ids, offsets)


def adagrad_kernel(grad_ref, accum_ref, table_hbm, new_table_hbm, new_accum_ref, tab, sem_in, sem_out):
    loads = [pltpu.make_async_copy(table_hbm.at[t], tab.at[t], sem_in.at[t]) for t in range(TBL)]
    stores = [pltpu.make_async_copy(tab.at[t], new_table_hbm.at[t], sem_out.at[t]) for t in range(TBL)]
    for copy in loads:
        copy.start()
    columns = jnp.swapaxes(accum_ref[...], 0, 1)
    fresh = columns
    for t in range(TBL):
        grad = grad_ref[t].astype(F32)
        accum = columns[:, t:t + 1] + jnp.sum(grad * grad, axis=1, keepdims=True) * (1.0 / E)
        fresh = jnp.where(iota((ROWS_DEV, TBL), 1) == t, accum, fresh)
        loads[t].wait()
        tab[t] = tab[t] - grad * (LEARN * lax.rsqrt(accum))
        stores[t].start()
    new_accum_ref[...] = jnp.swapaxes(fresh, 0, 1)
    for copy in stores:
        copy.wait()


def adagrad(grad, accum, table):
    vmem = pl.BlockSpec(memory_space=pltpu.VMEM)
    anywhere = pl.BlockSpec(memory_space=pl.ANY)
    return pl.pallas_call(
        adagrad_kernel,
        out_shape=(
            jax.ShapeDtypeStruct(table.shape, F32),
            jax.ShapeDtypeStruct(accum.shape, F32),
        ),
        in_specs=[vmem, vmem, anywhere],
        out_specs=(anywhere, vmem),
        scratch_shapes=[
            pltpu.VMEM((TBL, ROWS_DEV, E), F32),
            pltpu.SemaphoreType.DMA((TBL,)),
            pltpu.SemaphoreType.DMA((TBL,)),
        ],
        compiler_params=pltpu.CompilerParams(vmem_limit_bytes=40 * 1024 * 1024),
    )(grad, accum, table)


def on_device(cotangent, pooled, fm_weight, row_ids, bag_offsets, table, accum):
    grad = exchange(
        cotangent, pooled.reshape(B_DEV, TBL * E), fm_weight, row_ids[0], bag_offsets[0]
    )
    return adagrad(grad, accum, table)


def solution(mesh):
    return jax.shard_map(
        on_device,
        mesh=mesh,
        in_specs=(
            P(("rep", "shard"), None),
            P(("rep", "shard"), None, None),
            P(),
            P(("rep", "shard"), None, None),
            P(("rep", "shard"), None, None),
            P(None, "shard", None),
            P(None, "shard"),
        ),
        out_specs=(P(None, "shard", None), P(None, "shard")),
        check_vma=False,
    )
```

time: 325 us -> 94.3 us (0.29)
  the two profiles are of different devices: /device:TPU:8 before, /device:TPU:42 now
where the time goes in v1:
time: 94.3 us; the launch traced here: 94 us
  Pallas kernels  88.2 us (94%)
  local copies, waits for them, and re-layouts  5.1 us (5%)
    pallas_call x1, Pallas kernels, exchange(): pl.pallas_call(exchange_kernel, out_shape=jax.ShapeDtypeStruct((TBL, ROWS...  83.2 us
    unnamed x13, local copies, waits for them, and re-layouts  5.1 us
    pallas_call x1, Pallas kernels, adagrad(): pl.pallas_call(adagrad_kernel, out_shape=(jax.ShapeDtypeStruct(table.shap...  4.98 us

profile of v1, /device:TPU:42, one launch (start us, length us, event | category | flops | bytes accessed | tf_op | source)
XLA Modules:
  0.0 94.0 jit_solution(13173395417817002390)
XLA Ops:
  0.6 0.0 copy-start
  0.6 1.1 %copy.11 = bf16[16,8,8,128]{3,1,2,0:T(8,128)(2,1)S(1)} copy(bf16[16,8,8,128]{3,2,1,0:T(8,128)(2,1)} %bitcast.9) | data formatting | bytes 524288
  1.8 0.0 copy-start.1
  1.8 0.9 %copy-done.1 = bf16[128,1024]{1,0:T(8,128)(2,1)S(1)} copy-done((bf16[128,1024]{1,0:T(8,128)(2,1)S(1)}, bf16[128,1024]{1,0:T(8,128)(2,1)}, u32[]{:S(2)}) %copy-start.1) | copy-done | bytes 262168
  2.7 0.0 copy-start.2
  2.7 0.9 copy-done.2
  3.6 0.0 copy-start.4
  3.6 0.7 copy-done.4
  4.3 0.0 copy-start.5
  4.3 0.7 copy-done.5
  5.0 83.2 %shard_map.86.grad_ref = bf16[8,576,128]{2,1,0:T(8,128)(2,1)S(1)} custom-call(bf16[128,1024]{1,0:T(8,128)(2,1)S(1)} %copy-done.1, bf16[128,1024]{1,0:T(8,128)(2,1)S(1)} %bitcast.6, bf16[64,1024]{1,0:T(8,128)(2,1)S(1)} %copy-done.2, s32[8,192]{1,0:T(8,128)S(1)} %bitcast.7, s32[8,128]{1,0:T(8,128)S(1)} %bitcast.8), custom_call_target="tpu_custom_call" | custom-call | tf_op jit(solution)/shard_map/pallas_call | solution.py:293
  88.3 0.0 copy-done
  88.3 0.0 copy-start.3
  88.3 0.7 copy-done.3
  89.0 5.0 %shard_map.87 = (f32[8,576,128]{2,1,0:T(8,128)}, f32[8,576]{1,0:T(8,128)}) custom-call(bf16[8,576,128]{2,1,0:T(8,128)(2,1)S(1)} %shard_map.86.grad_ref, f32[8,576]{1,0:T(8,128)S(1)} %copy-done.3, f32[8,576,128]{2,1,0:T(8,128)S(1)} %copy-done), custom_call_target="tpu_custom_call" | custom-call | tf_op jit(solution)/shard_map/pallas_call | solution.py:345
Async XLA Ops:
  0.6 87.6 %copy-start = (f32[8,576,128]{2,1,0:T(8,128)S(1)}, f32[8,576,128]{2,1,0:T(8,128)}, u32[]{:S(2)}) copy-start(f32[8,576,128]{2,1,0:T(8,128)} %table_hbm.1) | copy-start | bytes 7077892
  1.8 1.0 %copy-start.1 = (bf16[128,1024]{1,0:T(8,128)(2,1)S(1)}, bf16[128,1024]{1,0:T(8,128)(2,1)}, u32[]{:S(2)}) copy-start(bf16[128,1024]{1,0:T(8,128)(2,1)} %cot_ref.1) | copy-start | bytes 786436
  2.7 0.9 copy-start.2
  3.6 0.7 copy-start.4
  4.3 0.7 copy-start.5
  88.3 0.7 copy-start.3

commit v2 on v0

v2 whole, which is shorter than its diff:
```python
import jax
import jax.numpy as jnp
from jax import lax
from jax.experimental import pallas as pl
from jax.experimental.pallas import tpu as pltpu
from jax.sharding import PartitionSpec as P

LEARN = 0.5
NX, NZ, NY = 4, 12, 8
GROUPS = 2 * NY
TBL, E, B_DEV, LOOK, CAP, ROWS_DEV = 8, 128, 128, 192, 24, 576
SLOTS = GROUPS * CAP
HEAD = 16
HALVES = TBL // NX
MSG = HALVES * CAP
CHUNKS = ((0, 32), (32, 16))
CUT = ROWS_DEV // 2
PIECE = ROWS_DEV // NZ
BF, F32, I32 = jnp.bfloat16, jnp.float32, jnp.int32
X_ORDER = (2, 1, 3, 0)
Y_ORDER = (4, 3, 5, 2, 6, 1, 7, 0)


def iota(shape, dim):
    return lax.broadcasted_iota(I32, shape, dim)


def dot(a, b, dims=((1,), (0,))):
    return lax.dot_general(a, b, (dims, ((), ())), preferred_element_type=F32)


def group_offsets(own):
    return [(dy, dc) for dy in Y_ORDER for dc in (0, 1) if own or (dy, dc) != (0, 0)]


def remote(src, dst, s, r, peer):
    return pltpu.make_async_remote_copy(
        src, dst, s, r, device_id=peer, device_id_type=pl.DeviceIdType.MESH
    )


def step_kernel(
    cot_hbm, x_hbm, w_hbm, ids_hbm, off_hbm, table_hbm, accum_hbm,
    out_ref, out_accum_ref,
    cot, x_in, x_f, w_v, ids_v, off_v, after_v, slot_v, acc_v, pg,
    head_out, head_in, send, recv, tq, tgt, total, zs, zin, g,
    load_sem, tab_sem, hd_s, hd_r, a_s, a_r, t_s, t_r, z_s, z_r, zg_s, zg_r, xg_s, xg_r, xf_s, xf_r,
):
    rep = lax.axis_index("rep")
    sh = lax.axis_index("shard")
    mx, mz = rep // NZ, rep % NZ
    my, mc = sh // 2, sh % 2

    def peer(dx, dy, dc):
        return {
            "rep": lax.rem(mx + dx, NX) * NZ + mz,
            "shard": lax.rem(my + dy, NY) * 2 + lax.rem(mc + dc, 2),
        }

    def z_peer(d):
        return {"rep": mx * NZ + lax.rem(mz + d, NZ), "shard": sh}

    def a2a_targets(dx):
        return [(dy, dc) for dy, dc in group_offsets(dx != 0)]

    loads = [
        pltpu.make_async_copy(src, dst, load_sem.at[n])
        for n, (src, dst) in enumerate(
            (
                (ids_hbm.at[0], ids_v), (off_hbm.at[0], off_v), (cot_hbm, cot), (w_hbm, w_v),
                (x_hbm, x_in), (accum_hbm, acc_v),
            )
        )
    ]
    for copy in loads:
        copy.start()
    table_load = pltpu.make_async_copy(table_hbm, out_ref, tab_sem)
    table_load.start()

    barrier = pltpu.get_barrier_semaphore()
    partners = [peer(dx, dy, dc) for dx in X_ORDER for dy, dc in a2a_targets(dx)]
    partners += [z_peer(d) for d in range(1, NZ)]
    for other in partners:
        pl.semaphore_signal(barrier, inc=1, device_id=other, device_id_type=pl.DeviceIdType.MESH)
    sends = []

    def start(*copies):
        for copy in copies:
            copy.start()
            sends.append(copy)

    loads[0].wait()
    loads[1].wait()
    ids = ids_v[...]
    owner = lax.shift_right_logical(ids * 7282, 22)
    local = ids - owner * ROWS_DEV + 1
    rel = ((lax.shift_right_logical(owner, 1) - my) & (NY - 1)) * 2 + ((owner & 1) ^ mc)
    member = jnp.concatenate(
        [(rel[t:t + 1, :] == iota((GROUPS, LOOK), 0)).astype(F32) for t in range(TBL)], axis=0
    )
    earlier = (iota((LOOK, LOOK), 0) < iota((LOOK, LOOK), 1)).astype(BF)
    before = dot(member.astype(BF), earlier)
    rank = jnp.sum((member * before).reshape(TBL, GROUPS, LOOK), axis=1).astype(I32)
    slot = rel * CAP + rank
    slot_v[...] = slot
    high = lax.shift_right_logical(local, 5).astype(F32)
    low = (local & 31).astype(F32)
    after = pltpu.roll(off_v[...], B_DEV - 1, 1)
    after_v[...] = jnp.where(iota((TBL, B_DEV), 1) == B_DEV - 1, LOOK, after)

    def spread(row):
        return (iota((SLOTS, LOOK), 0) == row).astype(BF)

    rows_h, rows_l = [], []
    for t in range(TBL):
        hl = jnp.where(iota((8, LOOK), 0) == 0, high[t:t + 1, :], low[t:t + 1, :]).astype(BF)
        placed = dot(hl, spread(slot[t:t + 1, :]), ((1,), (1,)))
        rows_h.append(placed[0:1, :])
        rows_l.append(placed[1:2, :])
    targets = jnp.concatenate(rows_h + rows_l, axis=0)
    mine = (iota((GROUPS, 1, SLOTS), 2) // CAP == iota((GROUPS, 1, SLOTS), 0)).astype(F32)
    fold = (iota((E, SLOTS), 1) % CAP == iota((E, SLOTS), 0)).astype(BF)
    apart = (targets[None] * mine).astype(BF).reshape(GROUPS * HEAD, SLOTS)
    heads = dot(apart, fold, ((1,), (1,))).astype(BF).reshape(GROUPS, HEAD, E)
    head_out[...] = heads
    head_in[0] = heads[0]

    def head_copy(dy, dc):
        o = dy * 2 + dc
        return remote(head_out.at[o], head_in.at[o], hd_s.at[o], hd_r.at[o], peer(0, dy, dc))

    swap = (iota((64, 64), 1) == (iota((64, 64), 0) % 8) * 8 + iota((64, 64), 0) // 8).astype(BF)
    loads[2].wait()
    loads[3].wait()
    w = w_v[...]
    w_t = dot(swap, w).astype(BF)
    sym = dot(cot[...], w, ((1,), (1,))) + dot(cot[...], w_t, ((1,), (1,)))
    loads[4].wait()
    x_f[...] = x_in[...].astype(F32).reshape(B_DEV * TBL, E)
    for i in range(TBL):
        acc = cot[:, i * E:(i + 1) * E].astype(F32)
        for j in range(TBL):
            acc = acc + sym[:, i * TBL + j:i * TBL + j + 1] * x_f[pl.ds(j, B_DEV, stride=TBL), :]
        pg[i] = acc.astype(BF)

    pl.semaphore_wait(barrier, len(partners))
    for dy, dc in group_offsets(False):
        start(head_copy(dy, dc))

    def table(h, d):
        return h * NX + lax.rem(mx + d, NX)

    def a2a(n, dx, dy, dc):
        o = dy * 2 + dc
        rows = pl.ds(*CHUNKS[n])
        return remote(
            send.at[dx, o, rows], recv.at[dx, o, rows], a_s.at[n, dx, o], a_r.at[n, dx, o], peer(dx, dy, dc)
        )

    kpos = iota((LOOK, B_DEV), 0)
    for dx in X_ORDER:
        parts = []
        for h in range(HALVES):
            t = table(h, dx)
            bags = (kpos >= off_v[pl.ds(t, 1), :]) & (kpos < after_v[pl.ds(t, 1), :])
            values = dot(bags.astype(BF), pg[t]).astype(BF)
            parts.append(dot(spread(slot_v[pl.ds(t, 1), :]), values).reshape(GROUPS, CAP, E))
        both = jnp.concatenate(parts, axis=1).astype(BF)
        send[dx] = both
        if dx == 0:
            recv[0, 0] = both[0]
        for dy, dc in a2a_targets(dx):
            start(a2a(0, dx, dy, dc))
    for n in range(1, len(CHUNKS)):
        for dx in X_ORDER:
            for dy, dc in a2a_targets(dx):
                start(a2a(n, dx, dy, dc))

    for dy, dc in group_offsets(False):
        head_copy(dy, dc).wait_recv()
    spots = dot(head_in[...].reshape(GROUPS * HEAD, E), fold).reshape(GROUPS, HEAD, SLOTS)
    got = jnp.sum(spots * mine, axis=0)
    got = got[0:TBL] * 32.0 + got[TBL:2 * TBL] - 1.0
    for q in range(NX):
        tq[q] = jnp.where(iota((8, SLOTS), 0) == 0, got[q:q + 1, :], got[q + NX:q + NX + 1, :])

    def target_copy(dx):
        return remote(tq.at[lax.rem(mx + dx, NX)], tgt.at[dx], t_s.at[dx], t_r.at[dx], peer(dx, 0, 0))

    for dx in X_ORDER[:-1]:
        start(target_copy(dx))
    tgt[0] = tq[mx]

    loads[5].wait()
    order = [(h, d) for h in range(HALVES) for d in range(NX)]
    columns = jnp.swapaxes(
        jnp.concatenate([acc_v[pl.ds(table(h, d), 1), :] for h, d in order], axis=0), 0, 1
    )
    for dx in X_ORDER[:-1]:
        target_copy(dx).wait_recv()

    def scatter(h):
        acc = None
        for dx in X_ORDER:
            for n in range(len(CHUNKS)):
                first = n == h if len(CHUNKS) > 1 else h == 0
                if first:
                    for dy, dc in a2a_targets(dx):
                        a2a(n, dx, dy, dc).wait_recv()
            lo, hi = (0, 32) if h == 0 else (16, 48)
            at = h * CAP - lo
            values = recv[dx, :, lo:hi, :].astype(F32)[:, at:at + CAP, :]
            values = values.reshape(SLOTS, E).astype(BF)
            onehot = (iota((ROWS_DEV, SLOTS), 0) == tgt[dx, h:h + 1, :].astype(I32)).astype(BF)
            part = dot(onehot, values)
            acc = part if acc is None else acc + part
        total[h] = acc
        zs[h] = acc.astype(BF)
        start(*z_reduce(h))

    upper, lower = pl.ds(0, CUT), pl.ds(CUT, CUT)
    right, left = peer(1, 0, 0), peer(NX - 1, 0, 0)
    own_rows = pl.ds(pl.multiple_of(mz * PIECE, PIECE), PIECE)

    def z_rows(d):
        return pl.ds(pl.multiple_of(lax.rem(mz + d, NZ) * PIECE, PIECE), PIECE)

    def z_reduce(h):
        return [
            remote(zs.at[h, z_rows(d)], zin.at[h, d], z_s.at[h, d], z_r.at[h, d], z_peer(d))
            for d in range(1, NZ)
        ]

    def z_gather(h, d, rows):
        at = g.at[table(h, 0), rows]
        return remote(at, at, zg_s.at[h, d], zg_r.at[h, d], z_peer(d))

    def x_gather(h, d, n):
        at = g.at[table(h, d), upper if n in (0, 3) else lower]
        return remote(at, at, xg_s.at[h, n], xg_r.at[h, n], right if n in (0, 2) else left)

    def x_forward(h, d, n):
        at = g.at[table(h, d), lower if n else upper]
        return remote(at, at, xf_s.at[h, n], xf_r.at[h, n], left if n else right)

    def z_sum(h):
        acc = total[h, own_rows]
        for d, copy in enumerate(z_reduce(h), start=1):
            copy.wait_recv()
            acc = acc + zin[h, d].astype(F32)
        g[table(h, 0), own_rows] = acc.astype(BF)
        start(*[z_gather(h, d, own_rows) for d in range(1, NZ)])

    def x_send(h):
        for d in range(1, NZ):
            z_gather(h, d, z_rows(NZ - d)).wait_recv()
        start(*[x_gather(h, 0, n) for n in range(4)])

    fresh = [columns]

    def update(h, d):
        t = table(h, d)
        grad = g[t].astype(F32)
        lane = h * NX + d
        accum = columns[:, lane:lane + 1] + jnp.sum(grad * grad, axis=1, keepdims=True) * (1.0 / E)
        fresh[0] = jnp.where(iota((ROWS_DEV, TBL), 1) == lane, accum, fresh[0])
        out_ref[t] = out_ref[t] - grad * (LEARN * lax.rsqrt(accum))

    def forward(h):
        x_gather(h, 3, 0).wait_recv()
        start(x_forward(h, 3, 0))
        x_gather(h, 1, 1).wait_recv()
        start(x_forward(h, 1, 1))

    def finish(h):
        update(h, 0)
        x_gather(h, 3, 2).wait_recv()
        update(h, 3)
        x_gather(h, 1, 3).wait_recv()
        update(h, 1)
        x_forward(h, 2, 0).wait_recv()
        x_forward(h, 2, 1).wait_recv()
        update(h, 2)

    scatter(0)
    z_sum(0)
    scatter(1)
    x_send(0)
    z_sum(1)
    forward(0)
    x_send(1)
    table_load.wait()
    forward(1)
    finish(0)
    finish(1)
    rows = jnp.swapaxes(fresh[0], 0, 1)
    for n, (h, d) in enumerate(order):
        out_accum_ref[pl.ds(table(h, d), 1), :] = rows[n:n + 1, :]
    for copy in sends:
        copy.wait_send()


def step(cot, pooled, w, ids, offsets, table, accum):
    vmem = pl.BlockSpec(memory_space=pltpu.VMEM)
    anywhere = pl.BlockSpec(memory_space=pl.ANY)
    dma = pltpu.SemaphoreType.DMA
    return pl.pallas_call(
        step_kernel,
        out_shape=(
            jax.ShapeDtypeStruct((TBL, ROWS_DEV, E), F32),
            jax.ShapeDtypeStruct((TBL, ROWS_DEV), F32),
        ),
        in_specs=[anywhere] * 7,
        out_specs=(vmem, vmem),
        scratch_shapes=[
            pltpu.VMEM((B_DEV, TBL * E), BF),
            pltpu.VMEM((B_DEV, TBL, E), BF),
            pltpu.VMEM((B_DEV * TBL, E), F32),
            pltpu.VMEM((TBL * TBL, TBL * E), BF),
            pltpu.VMEM((TBL, LOOK), I32),
            pltpu.VMEM((TBL, B_DEV), I32),
            pltpu.VMEM((TBL, B_DEV), I32),
            pltpu.VMEM((TBL, LOOK), I32),
            pltpu.VMEM((TBL, ROWS_DEV), F32),
            pltpu.VMEM((TBL, B_DEV, E), BF),
            pltpu.VMEM((GROUPS, HEAD, E), BF),
            pltpu.VMEM((GROUPS, HEAD, E), BF),
            pltpu.VMEM((NX, GROUPS, MSG, E), BF),
            pltpu.VMEM((NX, GROUPS, MSG, E), BF),
            pltpu.VMEM((NX, 8, SLOTS), F32),
            pltpu.VMEM((NX, 8, SLOTS), F32),
            pltpu.VMEM((HALVES, ROWS_DEV, E), F32),
            pltpu.VMEM((HALVES, ROWS_DEV, E), BF),
            pltpu.VMEM((HALVES, NZ, PIECE, E), BF),
            pltpu.VMEM((TBL, ROWS_DEV, E), BF),
            dma((6,)), dma,
            dma((GROUPS,)), dma((GROUPS,)),
            dma((len(CHUNKS), NX, GROUPS)), dma((len(CHUNKS), NX, GROUPS)),
            dma((NX,)), dma((NX,)),
            dma((HALVES, NZ)), dma((HALVES, NZ)),
            dma((HALVES, NZ)), dma((HALVES, NZ)),
            dma((HALVES, 4)), dma((HALVES, 4)),
            dma((HALVES, 2)), dma((HALVES, 2)),
        ],
        compiler_params=pltpu.CompilerParams(
            collective_id=0, has_side_effects=True, vmem_limit_bytes=56 * 1024 * 1024
        ),
    )(cot, pooled, w, ids, offsets, table, accum)


def solution(mesh):
    return jax.shard_map(
        step,
        mesh=mesh,
        in_specs=(
            P(("rep", "shard"), None),
            P(("rep", "shard"), None, None),
            P(),
            P(("rep", "shard"), None, None),
            P(("rep", "shard"), None, None),
            P(None, "shard", None),
            P(None, "shard"),
        ),
        out_specs=(P(None, "shard", None), P(None, "shard")),
        check_vma=False,
    )
```

time: 325 us -> 82.9 us (0.26)
  the two profiles are of different devices: /device:TPU:8 before, /device:TPU:4 now
where the time goes in v2:
time: 82.9 us; the launch traced here: 82.7 us
  Pallas kernels  78.2 us (94%)
  local copies, waits for them, and re-layouts  3.86 us (5%)
    pallas_call x1, Pallas kernels, step(): pl.pallas_call(step_kernel, out_shape=(jax.ShapeDtypeStruct((TBL, ROWS_DE...  78.2 us
    unnamed x4, local copies, waits for them, and re-layouts  3.86 us

profile of v2, /device:TPU:4, one launch (start us, length us, event | category | flops | bytes accessed | tf_op | source)
XLA Modules:
  0.0 82.7 jit_solution(2222790614033000601)
XLA Ops:
  0.6 78.2 %shard_map.86 = (f32[8,576,128]{2,1,0:T(8,128)}, f32[8,576]{1,0:T(8,128)}) custom-call(bf16[128,1024]{1,0:T(8,128)(2,1)} %cot_hbm.1, bf16[128,8,128]{2,1,0:T(8,128)(2,1)} %x_hbm.1, bf16[64,1024]{1,0:T(8,128)(2,1)} %w_hbm.1, s32[1,8,192]{2,1,0:T(8,128)} %ids_hbm.1, s32[1,8,128]{2,1,0:T(8,128)} %off_hbm.1, f32[8,576,128]{2,1,0:T(8,128)} %table_hbm.1, ...), custom_call_target="tpu_custom_call" | custom-call | tf_op jit(solution)/shard_map/pallas_call | solution.py:307
  78.8 0.0 copy-start
  78.8 3.2 %copy.11 = f32[8,576,128]{2,1,0:T(8,128)} copy(f32[8,576,128]{2,1,0:T(8,128)} %get-tuple-element.4) | data formatting | bytes 4718592
  82.1 0.0 copy-done
  82.1 0.6 copy.12
Async XLA Ops:
  78.8 3.3 %copy-start = (f32[8,576]{1,0:T(8,128)S(1)}, f32[8,576]{1,0:T(8,128)}, u32[]{:S(2)}) copy-start(f32[8,576]{1,0:T(8,128)} %get-tuple-element.5) | copy-start | bytes 55300

commit v3 on v2

--- a/solution.py
+++ b/solution.py
@@ -14,11 +14,12 @@
 HALVES = TBL // NX
 MSG = HALVES * CAP
 CHUNKS = ((0, 32), (32, 16))
-CUT = ROWS_DEV // 2
 PIECE = ROWS_DEV // NZ
 BF, F32, I32 = jnp.bfloat16, jnp.float32, jnp.int32
 X_ORDER = (2, 1, 3, 0)
 Y_ORDER = (4, 3, 5, 2, 6, 1, 7, 0)
+Z_ORDER = (6, 5, 7, 4, 8, 3, 9, 2, 10, 1, 11)
+PARTS = ((0, 1), (1, 3), (9, 3), (4, 5))
 
 
 def iota(shape, dim):
@@ -40,11 +41,11 @@
 
 
 def step_kernel(
-    cot_hbm, x_hbm, w_hbm, ids_hbm, off_hbm, table_hbm, accum_hbm,
+    cot_hbm, x_hbm, w_hbm, ids_hbm, off_hbm, accum_hbm,
     out_ref, out_accum_ref,
     cot, x_in, x_f, w_v, ids_v, off_v, after_v, slot_v, acc_v, pg,
     head_out, head_in, send, recv, tq, tgt, total, zs, zin, g,
-    load_sem, tab_sem, hd_s, hd_r, a_s, a_r, t_s, t_r, z_s, z_r, zg_s, zg_r, xg_s, xg_r, xf_s, xf_r,
+    load_sem, hd_s, hd_r, a_s, a_r, t_s, t_r, z_s, z_r, zg_s, zg_r, xg_s, xg_r,
 ):
     rep = lax.axis_index("rep")
     sh = lax.axis_index("shard")
@@ -74,8 +75,6 @@
     ]
     for copy in loads:
         copy.start()
-    table_load = pltpu.make_async_copy(table_hbm, out_ref, tab_sem)
-    table_load.start()
 
     barrier = pltpu.get_barrier_semaphore()
     partners = [peer(dx, dy, dc) for dx in X_ORDER for dy, dc in a2a_targets(dx)]
@@ -218,80 +217,69 @@
         zs[h] = acc.astype(BF)
         start(*z_reduce(h))
 
-    upper, lower = pl.ds(0, CUT), pl.ds(CUT, CUT)
-    right, left = peer(1, 0, 0), peer(NX - 1, 0, 0)
     own_rows = pl.ds(pl.multiple_of(mz * PIECE, PIECE), PIECE)
-
-    def z_rows(d):
-        return pl.ds(pl.multiple_of(lax.rem(mz + d, NZ) * PIECE, PIECE), PIECE)
 
     def z_reduce(h):
         return [
-            remote(zs.at[h, z_rows(d)], zin.at[h, d], z_s.at[h, d], z_r.at[h, d], z_peer(d))
-            for d in range(1, NZ)
+            remote(
+                zs.at[h, pl.ds(pl.multiple_of(lax.rem(mz + d, NZ) * PIECE, PIECE), PIECE)],
+                zin.at[h, d], z_s.at[h, d], z_r.at[h, d], z_peer(d),
+            )
+            for d in Z_ORDER
         ]
 
-    def z_gather(h, d, rows):
-        at = g.at[table(h, 0), rows]
-        return remote(at, at, zg_s.at[h, d], zg_r.at[h, d], z_peer(d))
-
-    def x_gather(h, d, n):
-        at = g.at[table(h, d), upper if n in (0, 3) else lower]
-        return remote(at, at, xg_s.at[h, n], xg_r.at[h, n], right if n in (0, 2) else left)
-
-    def x_forward(h, d, n):
-        at = g.at[table(h, d), lower if n else upper]
-        return remote(at, at, xf_s.at[h, n], xf_r.at[h, n], left if n else right)
+    def z_gather(h, d):
+        t = table(h, 0)
+        return remote(g.at[t, 0], g.at[t, NZ - d], zg_s.at[h, d], zg_r.at[h, d], z_peer(d))
+
+    def x_gather(h, n, dx, d):
+        at = g.at[table(h, d), pl.ds(*PARTS[n])]
+        return remote(at, at, xg_s.at[h, n, dx], xg_r.at[h, n, dx], peer(dx, 0, 0))
 
     def z_sum(h):
         acc = total[h, own_rows]
-        for d, copy in enumerate(z_reduce(h), start=1):
+        for d, copy in reversed(list(zip(Z_ORDER, z_reduce(h)))):
             copy.wait_recv()
             acc = acc + zin[h, d].astype(F32)
-        g[table(h, 0), own_rows] = acc.astype(BF)
-        start(*[z_gather(h, d, own_rows) for d in range(1, NZ)])
-
-    def x_send(h):
-        for d in range(1, NZ):
-            z_gather(h, d, z_rows(NZ - d)).wait_recv()
-        start(*[x_gather(h, 0, n) for n in range(4)])
+        g[table(h, 0), 0] = acc.astype(BF)
+        start(*[z_gather(h, d) for d in Z_ORDER])
+        x_send(h, 0)
+
+    def x_send(h, n):
+        first, count = PARTS[n]
+        for e in range(first, first + count):
+            if e:
+                remote(g.at[table(h, 0), 0], g.at[table(h, 0), e], zg_s.at[h, NZ - e], zg_r.at[h, NZ - e], z_peer(e)).wait_recv()
+        start(*[x_gather(h, n, dx, 0) for dx in X_ORDER[:-1]])
 
     fresh = [columns]
 
     def update(h, d):
         t = table(h, d)
-        grad = g[t].astype(F32)
+        grad = jnp.concatenate([g[t, lax.rem(w_at - mz + NZ, NZ)] for w_at in range(NZ)], axis=0).astype(F32)
         lane = h * NX + d
         accum = columns[:, lane:lane + 1] + jnp.sum(grad * grad, axis=1, keepdims=True) * (1.0 / E)
         fresh[0] = jnp.where(iota((ROWS_DEV, TBL), 1) == lane, accum, fresh[0])
-        out_ref[t] = out_ref[t] - grad * (LEARN * lax.rsqrt(accum))
-
-    def forward(h):
-        x_gather(h, 3, 0).wait_recv()
-        start(x_forward(h, 3, 0))
-        x_gather(h, 1, 1).wait_recv()
-        start(x_forward(h, 1, 1))
+        out_ref[t] = (grad * (LEARN * lax.rsqrt(accum))).astype(BF)
 
     def finish(h):
         update(h, 0)
-        x_gather(h, 3, 2).wait_recv()
-        update(h, 3)
-        x_gather(h, 1, 3).wait_recv()
-        update(h, 1)
-        x_forward(h, 2, 0).wait_recv()
-        x_forward(h, 2, 1).wait_recv()
-        update(h, 2)
+        for dx in (1, 3, 2):
+            for n in range(len(PARTS)):
+                x_gather(h, n, dx, NX - dx).wait_recv()
+            update(h, NX - dx)
 
     scatter(0)
+    scatter(1)
     z_sum(0)
-    scatter(1)
-    x_send(0)
+    x_send(0, 1)
+    x_send(0, 2)
     z_sum(1)
-    forward(0)
-    x_send(1)
-    table_load.wait()
-    forward(1)
+    x_send(0, 3)
+    x_send(1, 1)
+    x_send(1, 2)
     finish(0)
+    x_send(1, 3)
     finish(1)
     rows = jnp.swapaxes(fresh[0], 0, 1)
     for n, (h, d) in enumerate(order):
@@ -300,17 +288,17 @@
         copy.wait_send()
 
 
-def step(cot, pooled, w, ids, offsets, table, accum):
+def row_steps(cot, pooled, w, ids, offsets, accum):
     vmem = pl.BlockSpec(memory_space=pltpu.VMEM)
     anywhere = pl.BlockSpec(memory_space=pl.ANY)
     dma = pltpu.SemaphoreType.DMA
     return pl.pallas_call(
         step_kernel,
         out_shape=(
-            jax.ShapeDtypeStruct((TBL, ROWS_DEV, E), F32),
+            jax.ShapeDtypeStruct((TBL, ROWS_DEV, E), BF),
             jax.ShapeDtypeStruct((TBL, ROWS_DEV), F32),
         ),
-        in_specs=[anywhere] * 7,
+        in_specs=[anywhere] * 6,
         out_specs=(vmem, vmem),
         scratch_shapes=[
             pltpu.VMEM((B_DEV, TBL * E), BF),
@@ -332,20 +320,24 @@
             pltpu.VMEM((HALVES, ROWS_DEV, E), F32),
             pltpu.VMEM((HALVES, ROWS_DEV, E), BF),
             pltpu.VMEM((HALVES, NZ, PIECE, E), BF),
-            pltpu.VMEM((TBL, ROWS_DEV, E), BF),
-            dma((6,)), dma,
+            pltpu.VMEM((TBL, NZ, PIECE, E), BF),
+            dma((6,)),
             dma((GROUPS,)), dma((GROUPS,)),
             dma((len(CHUNKS), NX, GROUPS)), dma((len(CHUNKS), NX, GROUPS)),
             dma((NX,)), dma((NX,)),
             dma((HALVES, NZ)), dma((HALVES, NZ)),
             dma((HALVES, NZ)), dma((HALVES, NZ)),
-            dma((HALVES, 4)), dma((HALVES, 4)),
-            dma((HALVES, 2)), dma((HALVES, 2)),
+            dma((HALVES, len(PARTS), NX)), dma((HALVES, len(PARTS), NX)),
         ],
         compiler_params=pltpu.CompilerParams(
             collective_id=0, has_side_effects=True, vmem_limit_bytes=56 * 1024 * 1024
         ),
-    )(cot, pooled, w, ids, offsets, table, accum)
+    )(cot, pooled, w, ids, offsets, accum)
+
+
+def step(cot, pooled, w, ids, offsets, table, accum):
+    delta, new_accum = row_steps(cot, pooled, w, ids, offsets, accum)
+    return table - delta.astype(F32), new_accum
 
 
 def solution(mesh):

time: 82.9 us -> 78.3 us (0.945)
  the two profiles are of different devices: /device:TPU:4 before, /device:TPU:10 now
where the time goes in v3:
time: 78.3 us; the launch traced here: 78.1 us
  Pallas kernels  73.3 us (94%)
  other arithmetic  3.59 us (5%)
    pallas_call x1, Pallas kernels, row_steps(): pl.pallas_call(step_kernel, out_shape=(jax.ShapeDtypeStruct((TBL, ROWS_DE...  73.3 us
    sub x1, other arithmetic, step(): return (table - delta.astype(F32), new_accum)  3.59 us

profile of v3, /device:TPU:10, one launch (start us, length us, event | category | flops | bytes accessed | tf_op | source)
XLA Modules:
  0.0 78.1 jit_solution(12072096655951730248)
XLA Ops:
  0.6 73.3 %shard_map.86 = (bf16[8,576,128]{2,1,0:T(8,128)(2,1)}, f32[8,576]{1,0:T(8,128)}) custom-call(bf16[128,1024]{1,0:T(8,128)(2,1)} %cot_hbm.1, bf16[128,8,128]{2,1,0:T(8,128)(2,1)} %x_hbm.1, bf16[64,1024]{1,0:T(8,128)(2,1)} %w_hbm.1, s32[1,8,192]{2,1,0:T(8,128)} %ids_hbm.1, s32[1,8,128]{2,1,0:T(8,128)} %off_hbm.1, f32[8,576]{1,0:T(8,128)} %accum_hbm.1), custom_call_target="tpu_custom_call" | custom-call | tf_op jit(solution)/shard_map/pallas_call | solution.py:295
  73.9 0.0 copy-start
  73.9 3.6 %convert_subtract_fusion = f32[8,576,128]{2,1,0:T(8,128)} fusion(f32[8,576,128]{2,1,0:T(8,128)} %param.12, bf16[8,576,128]{2,1,0:T(8,128)(2,1)} %get-tuple-element.4), kind=kLoop, calls=%fused_computation | loop fusion | flops 1179648 | bytes 5898240 | tf_op jit(solution)/shard_map/sub | solution.py:340
  77.5 0.0 copy-done
  77.5 0.6 copy.10
Async XLA Ops:
  73.9 3.6 %copy-start = (f32[8,576]{1,0:T(8,128)S(1)}, f32[8,576]{1,0:T(8,128)}, u32[]{:S(2)}) copy-start(f32[8,576]{1,0:T(8,128)} %get-tuple-element.9) | copy-start | bytes 55300

commit v4 on v3

--- a/solution.py
+++ b/solution.py
@@ -18,7 +18,7 @@
 BF, F32, I32 = jnp.bfloat16, jnp.float32, jnp.int32
 X_ORDER = (2, 1, 3, 0)
 Y_ORDER = (4, 3, 5, 2, 6, 1, 7, 0)
-Z_ORDER = (6, 5, 7, 4, 8, 3, 9, 2, 10, 1, 11)
+Z_ORDER = (1, 11, 2, 10, 3, 9, 4, 8, 5, 7, 6)
 PARTS = ((0, 1), (1, 3), (9, 3), (4, 5))
 
 
@@ -42,10 +42,10 @@
 
 def step_kernel(
     cot_hbm, x_hbm, w_hbm, ids_hbm, off_hbm, accum_hbm,
-    out_ref, out_accum_ref,
+    out_hbm, out_accum_hbm,
     cot, x_in, x_f, w_v, ids_v, off_v, after_v, slot_v, acc_v, pg,
     head_out, head_in, send, recv, tq, tgt, total, zs, zin, g,
-    load_sem, hd_s, hd_r, a_s, a_r, t_s, t_r, z_s, z_r, zg_s, zg_r, xg_s, xg_r,
+    load_sem, hd_s, hd_r, a_s, a_r, t_s, t_r, z_s, z_r, zg_s, zg_r, xg_s, xg_r, out_ref, fresh_v, out_sem, fresh_sem,
 ):
     rep = lax.axis_index("rep")
     sh = lax.axis_index("shard")
@@ -238,7 +238,7 @@
 
     def z_sum(h):
         acc = total[h, own_rows]
-        for d, copy in reversed(list(zip(Z_ORDER, z_reduce(h)))):
+        for d, copy in list(zip(Z_ORDER, z_reduce(h))):
             copy.wait_recv()
             acc = acc + zin[h, d].astype(F32)
         g[table(h, 0), 0] = acc.astype(BF)
@@ -252,7 +252,7 @@
                 remote(g.at[table(h, 0), 0], g.at[table(h, 0), e], zg_s.at[h, NZ - e], zg_r.at[h, NZ - e], z_peer(e)).wait_recv()
         start(*[x_gather(h, n, dx, 0) for dx in X_ORDER[:-1]])
 
-    fresh = [columns]
+    fresh, stores = [columns], []
 
     def update(h, d):
         t = table(h, d)
@@ -261,9 +261,11 @@
         accum = columns[:, lane:lane + 1] + jnp.sum(grad * grad, axis=1, keepdims=True) * (1.0 / E)
         fresh[0] = jnp.where(iota((ROWS_DEV, TBL), 1) == lane, accum, fresh[0])
         out_ref[t] = (grad * (LEARN * lax.rsqrt(accum))).astype(BF)
+        store = pltpu.make_async_copy(out_ref.at[t], out_hbm.at[t], out_sem.at[lane])
+        store.start()
+        stores.append(store)
 
     def finish(h):
-        update(h, 0)
         for dx in (1, 3, 2):
             for n in range(len(PARTS)):
                 x_gather(h, n, dx, NX - dx).wait_recv()
@@ -278,18 +280,23 @@
     x_send(0, 3)
     x_send(1, 1)
     x_send(1, 2)
+    update(0, 0)
     finish(0)
     x_send(1, 3)
+    update(1, 0)
     finish(1)
     rows = jnp.swapaxes(fresh[0], 0, 1)
     for n, (h, d) in enumerate(order):
-        out_accum_ref[pl.ds(table(h, d), 1), :] = rows[n:n + 1, :]
+        fresh_v[pl.ds(table(h, d), 1), :] = rows[n:n + 1, :]
+    stores.append(pltpu.make_async_copy(fresh_v, out_accum_hbm, fresh_sem))
+    stores[-1].start()
     for copy in sends:
         copy.wait_send()
+    for store in stores:
+        store.wait()
 
 
 def row_steps(cot, pooled, w, ids, offsets, accum):
-    vmem = pl.BlockSpec(memory_space=pltpu.VMEM)
     anywhere = pl.BlockSpec(memory_space=pl.ANY)
     dma = pltpu.SemaphoreType.DMA
     return pl.pallas_call(
@@ -299,7 +306,7 @@
             jax.ShapeDtypeStruct((TBL, ROWS_DEV), F32),
         ),
         in_specs=[anywhere] * 6,
-        out_specs=(vmem, vmem),
+        out_specs=(anywhere, anywhere),
         scratch_shapes=[
             pltpu.VMEM((B_DEV, TBL * E), BF),
             pltpu.VMEM((B_DEV, TBL, E), BF),
@@ -328,6 +335,8 @@
             dma((HALVES, NZ)), dma((HALVES, NZ)),
             dma((HALVES, NZ)), dma((HALVES, NZ)),
             dma((HALVES, len(PARTS), NX)), dma((HALVES, len(PARTS), NX)),
+            pltpu.VMEM((TBL, ROWS_DEV, E), BF), pltpu.VMEM((TBL, ROWS_DEV), F32),
+            dma((TBL,)), dma,
         ],
         compiler_params=pltpu.CompilerParams(
             collective_id=0, has_side_effects=True, vmem_limit_bytes=56 * 1024 * 1024
@@ -335,9 +344,57 @@
     )(cot, pooled, w, ids, offsets, accum)
 
 
+def apply_kernel(
+    delta_hbm, table_hbm, accum_hbm, new_table_hbm, new_accum_hbm,
+    delta, tab, acc_v, d_sem, t_sem, o_sem, a_sem,
+):
+    acc_in = pltpu.make_async_copy(accum_hbm, acc_v, a_sem.at[0])
+    acc_out = pltpu.make_async_copy(acc_v, new_accum_hbm, a_sem.at[1])
+    stores = []
+    acc_in.start()
+    loads = []
+    for t in range(TBL):
+        pair = (
+            pltpu.make_async_copy(delta_hbm.at[t], delta.at[t], d_sem.at[t]),
+            pltpu.make_async_copy(table_hbm.at[t], tab.at[t], t_sem.at[t]),
+        )
+        for copy in pair:
+            copy.start()
+        loads.append(pair)
+    acc_in.wait()
+    acc_out.start()
+    for t in range(TBL):
+        for copy in loads[t]:
+            copy.wait()
+        tab[t] = tab[t] - delta[t].astype(F32)
+        store = pltpu.make_async_copy(tab.at[t], new_table_hbm.at[t], o_sem.at[t])
+        store.start()
+        stores.append(store)
+    acc_out.wait()
+    for store in stores:
+        store.wait()
+
+
 def step(cot, pooled, w, ids, offsets, table, accum):
     delta, new_accum = row_steps(cot, pooled, w, ids, offsets, accum)
-    return table - delta.astype(F32), new_accum
+    anywhere = pl.BlockSpec(memory_space=pl.ANY)
+    dma = pltpu.SemaphoreType.DMA
+    return pl.pallas_call(
+        apply_kernel,
+        out_shape=(
+            jax.ShapeDtypeStruct((TBL, ROWS_DEV, E), F32),
+            jax.ShapeDtypeStruct((TBL, ROWS_DEV), F32),
+        ),
+        in_specs=[anywhere] * 3,
+        out_specs=(anywhere, anywhere),
+        scratch_shapes=[
+            pltpu.VMEM((TBL, ROWS_DEV, E), BF),
+            pltpu.VMEM((TBL, ROWS_DEV, E), F32),
+            pltpu.VMEM((TBL, ROWS_DEV), F32),
+            dma((TBL,)), dma((TBL,)), dma((TBL,)), dma((2,)),
+        ],
+        compiler_params=pltpu.CompilerParams(vmem_limit_bytes=56 * 1024 * 1024),
+    )(delta, table, new_accum)
 
 
 def solution(mesh):

time: 78.3 us -> 75.6 us (0.966)
  the two profiles are of different devices: /device:TPU:10 before, /device:TPU:16 now
where the time goes in v4:
time: 75.6 us; the launch traced here: 75.4 us
  Pallas kernels  74.8 us (99%)
    pallas_call x1, Pallas kernels, row_steps(): pl.pallas_call(step_kernel, out_shape=(jax.ShapeDtypeStruct((TBL, ROWS_DE...  71.4 us
    pallas_call x1, Pallas kernels, step(): pl.pallas_call(apply_kernel, out_shape=(jax.ShapeDtypeStruct((TBL, ROWS_D...  3.36 us

profile of v4, /device:TPU:16, one launch (start us, length us, event | category | flops | bytes accessed | tf_op | source)
XLA Modules:
  0.0 75.4 jit_solution(12014673477038515348)
XLA Ops:
  0.6 71.4 %shard_map.86 = (bf16[8,576,128]{2,1,0:T(8,128)(2,1)}, f32[8,576]{1,0:T(8,128)}) custom-call(bf16[128,1024]{1,0:T(8,128)(2,1)} %cot_hbm.1, bf16[128,8,128]{2,1,0:T(8,128)(2,1)} %x_hbm.1, bf16[64,1024]{1,0:T(8,128)(2,1)} %w_hbm.1, s32[1,8,192]{2,1,0:T(8,128)} %ids_hbm.1, s32[1,8,128]{2,1,0:T(8,128)} %off_hbm.1, f32[8,576]{1,0:T(8,128)} %accum_hbm.1), custom_call_target="tpu_custom_call" | custom-call | tf_op jit(solution)/shard_map/pallas_call | solution.py:302
  72.1 3.4 %shard_map.87 = (f32[8,576,128]{2,1,0:T(8,128)}, f32[8,576]{1,0:T(8,128)}) custom-call(bf16[8,576,128]{2,1,0:T(8,128)(2,1)} %get-tuple-element.4.delta_hbm, f32[8,576,128]{2,1,0:T(8,128)} %table_hbm.1, f32[8,576]{1,0:T(8,128)} %get-tuple-element.5.accum_hbm), custom_call_target="tpu_custom_call" | custom-call | tf_op jit(solution)/shard_map/pallas_call | solution.py:382

commit v5 on v4

--- a/solution.py
+++ b/solution.py
@@ -77,8 +77,12 @@
         copy.start()
 
     barrier = pltpu.get_barrier_semaphore()
-    partners = [peer(dx, dy, dc) for dx in X_ORDER for dy, dc in a2a_targets(dx)]
-    partners += [z_peer(d) for d in range(1, NZ)]
+    ranked = [
+        (min(dx, NX - dx) + min(dy, NY - dy), dx, dy, dc) for dx in X_ORDER for dy, dc in a2a_targets(dx)
+    ]
+    ranked += [(min(d, NZ - d), d) for d in range(1, NZ)]
+    ranked.sort(key=lambda entry: -entry[0])
+    partners = [z_peer(entry[1]) if len(entry) == 2 else peer(*entry[1:]) for entry in ranked]
     for other in partners:
         pl.semaphore_signal(barrier, inc=1, device_id=other, device_id_type=pl.DeviceIdType.MESH)
     sends = []

time: 75.6 us -> 74.9 us (level)
  the two profiles are of different devices: /device:TPU:16 before, /device:TPU:2 now
where the time goes in v5:
time: 74.9 us; the launch traced here: 74.7 us
  Pallas kernels  74.1 us (99%)
    pallas_call x1, Pallas kernels, row_steps(): pl.pallas_call(step_kernel, out_shape=(jax.ShapeDtypeStruct((TBL, ROWS_DE...  70.7 us
    pallas_call x1, Pallas kernels, step(): pl.pallas_call(apply_kernel, out_shape=(jax.ShapeDtypeStruct((TBL, ROWS_D...  3.36 us

profile of v5, /device:TPU:2, one launch (start us, length us, event | category | flops | bytes accessed | tf_op | source)
XLA Modules:
  0.0 74.7 jit_solution(616572395237752138)
XLA Ops:
  0.6 70.7 %shard_map.86 = (bf16[8,576,128]{2,1,0:T(8,128)(2,1)}, f32[8,576]{1,0:T(8,128)}) custom-call(bf16[128,1024]{1,0:T(8,128)(2,1)} %cot_hbm.1, bf16[128,8,128]{2,1,0:T(8,128)(2,1)} %x_hbm.1, bf16[64,1024]{1,0:T(8,128)(2,1)} %w_hbm.1, s32[1,8,192]{2,1,0:T(8,128)} %ids_hbm.1, s32[1,8,128]{2,1,0:T(8,128)} %off_hbm.1, f32[8,576]{1,0:T(8,128)} %accum_hbm.1), custom_call_target="tpu_custom_call" | custom-call | tf_op jit(solution)/shard_map/pallas_call | solution.py:306
  71.3 3.4 %shard_map.87 = (f32[8,576,128]{2,1,0:T(8,128)}, f32[8,576]{1,0:T(8,128)}) custom-call(bf16[8,576,128]{2,1,0:T(8,128)(2,1)} %get-tuple-element.4.delta_hbm, f32[8,576,128]{2,1,0:T(8,128)} %table_hbm.1, f32[8,576]{1,0:T(8,128)} %get-tuple-element.5.accum_hbm), custom_call_target="tpu_custom_call" | custom-call | tf_op jit(solution)/shard_map/pallas_call | solution.py:386
